TPU v7x, 32 devices: a whole 2x2x4 slice. The times are simulated.
32 devices in a mesh: seg: 4 (over y, core), sec: 8 (over z, x).
Axes of the slice: x: 2, y: 2, z: 4, core: 2. Of those that a mesh axis runs over, the one named last changes fastest.
Arguments:
- psi_init: float32 [4, 8, 256, 256], P('seg', 'sec'), may hold values from -6 to 6
- boundary_env: float32 [8, 18, 256, 256], P('sec')
- right_env: float32 [4, 8, 18, 256, 256], P('seg', 'sec')
- transfer_blocks: float32 [4, 8, 256, 256], P('seg', 'sec')
- transfer_mix: float32 [4, 18, 18], P('seg')
- hop_left: float32 [4, 8, 256, 256], P('seg', 'sec'), may hold values from -0.75 to 0.75
- hop_right: float32 [4, 8, 256, 256], P('seg', 'sec'), may hold values from -0.75 to 0.75
- block_sizes: int32 [4, 2, 8], P('seg'), may hold values from 64 to 256, as said below
- sources: int32 [4, 8], P('seg'), may hold values from 0 to 7, each once within a row
Outputs:
- state: float32 [4, 8, 256, 256], P('seg', 'sec')
Inputs may be any that keep to these rules, and one draw needn't show every extreme that they name: `sources`: each block number appears once in a segment's list. `block_sizes`: each segment has a block with 256 live rows and one with 256 live columns.
All inputs are finite; a program needn't handle non-finite values.
Results may differ from a plain program's by a relative error of at most 0.0003.
Values sent between devices are 32-bit elements; how exact they have to be, the bound alone decides.
A program may use at most 128 MiB of HBM per device.

v0:
```python
import jax
import jax.numpy as jnp
from jax import lax
from jax.sharding import PartitionSpec as P

DAV = 2


HIGH = lax.Precision.HIGHEST
EPSILON = 1e-06


def passed_along(value, axis, steps):
    count = lax.axis_size(axis)
    initial, last = (max(0, -steps), min(count, count - steps))
    return lax.ppermute(value, axis, [(source, source + steps) for source in range(initial, last)])


def product(left, right):
    return jnp.matmul(left, right, precision=HIGH)


def combine(earlier, later):
    return (product(earlier[0], later[0]), product(earlier[1], later[1]))


def norm_total(vector):
    return lax.psum(jnp.sum(vector * vector), "sec")


def per_device(
    psi_init,
    boundary_env,
    right_env,
    transfer_blocks,
    transfer_mix,
    hop_left,
    hop_right,
    block_sizes,
    sources,
):
    initial = psi_init[0]
    right_side = right_env[0]
    own_blocks = transfer_blocks[0]
    own_mix = transfer_mix[0]
    left_hop = hop_left[0]
    right_hop = hop_right[0]
    all_sizes = block_sizes[0]
    all_sources = sources[0]
    local_blocks = initial.shape[0]
    block_width = initial.shape[1]
    channels = own_mix.shape[0]
    sector_count = lax.axis_size("sec")
    first_block = lax.axis_index("sec") * local_blocks
    eye_mix = jnp.eye(channels, dtype=jnp.float32)
    eye_blocks = jnp.broadcast_to(jnp.eye(block_width, dtype=jnp.float32), own_blocks.shape)
    prefix_mix, prefix_blocks = (eye_mix, eye_blocks)
    leading = lax.axis_index("seg") == 0
    for hop_index in range(lax.axis_size("seg") - 1):
        carry_mix, carry_blocks = combine((prefix_mix, prefix_blocks), (own_mix, own_blocks))
        got_mix, got_blocks = passed_along((carry_mix, carry_blocks), "seg", 1)
        prefix_mix = jnp.where(leading, eye_mix, got_mix)
        prefix_blocks = jnp.where(leading, eye_blocks, got_blocks)
    turned = product(
        product(jnp.swapaxes(prefix_blocks, 1, 2)[:, None], boundary_env), prefix_blocks[:, None]
    )
    left_env = jnp.einsum("vw,bvij->bwij", prefix_mix, turned, precision=HIGH)
    live_sizes = lax.dynamic_slice_in_dim(all_sizes, first_block, local_blocks, 1)
    wanted = lax.dynamic_slice_in_dim(all_sources, first_block, local_blocks, 0)
    places = lax.broadcasted_iota(jnp.int32, (1, block_width), 1)
    row_live = (places < live_sizes[0][:, None]).astype(jnp.float32)
    col_live = (places < live_sizes[1][:, None]).astype(jnp.float32)
    masking = row_live[:, :, None] * col_live[:, None, :]
    diagonal = jnp.einsum(
        "bwi,bwj->bij",
        jnp.diagonal(left_env, axis1=2, axis2=3),
        jnp.diagonal(right_side, axis1=2, axis2=3),
        precision=HIGH,
    )
    vector = masking * initial
    vector = vector / jnp.sqrt(norm_total(vector) + EPSILON)
    for turn_index in range(DAV):
        local_part = jnp.sum(product(product(left_env, vector[:, None]), right_side), axis=1)
        moving = product(vector, right_hop)
        shard_piece = lax.all_gather(moving, "sec", axis=0, tiled=True)
        global_ids = lax.broadcasted_iota(jnp.int32, (1, shard_piece.shape[0]), 1)
        chooser = (wanted[:, None] == global_ids).astype(jnp.float32)
        regrouped = jnp.zeros_like(moving) + jnp.einsum(
            "ji,ipc->jpc", chooser, shard_piece, precision=HIGH
        )
        image_vec = masking * (local_part + product(left_hop, regrouped))
        rayleigh = lax.psum(jnp.sum(vector * image_vec), "sec")
        residue = image_vec - rayleigh * vector
        shifted = diagonal - rayleigh
        update = vector - residue * shifted / (shifted * shifted + 1.0)
        vector = update / jnp.sqrt(norm_total(update) + EPSILON)
    cells = float(local_blocks * sector_count * block_width * block_width)
    return (vector * jnp.sqrt(jnp.float32(cells)))[None]


def solution(mesh):
    return jax.shard_map(
        per_device,
        mesh=mesh,
        in_specs=(
            P("seg", "sec", None, None),
            P("sec", None, None, None),
            P("seg", "sec", None, None, None),
            P("seg", "sec", None, None),
            P("seg", None, None),
            P("seg", "sec", None, None),
            P("seg", "sec", None, None),
            P("seg", None, None),
            P("seg", None),
        ),
        out_specs=P("seg", "sec", None, None),
        check_vma=False,
    )
```

profile of v0, /device:TPU:0, one launch (start us, length us, event | category | flops | bytes accessed | tf_op | source)
XLA Modules:
  0.0 281.5 jit_solution(10141005877216989702)
XLA Ops:
  11.3 2.4 collective-permute-start
  13.6 23.1 %psum.35 = f32[]{:T(128)} all-reduce(f32[]{:T(128)} %fusion.53), channel_id=1, replica_groups=mesh['seg'=4,'sec'=8] {'sec'}, use_global_device_ids=true, to_apply=%region_1.2 | all-reduce | flops 1 | bytes 8 | tf_op jit(solution)/shard_map/psum | solution.py:28
  37.5 2.2 fusion.45
  42.3 4.3 %collective-permute-start.3 = (f32[18,18]{1,0:T(8,128)S(1)}, f32[18,18]{1,0:T(8,128)S(1)}, u32[]{:S(2)}, u32[]{:S(2)}) collective-permute-start(f32[18,18]{1,0:T(8,128)S(1)} %fusion.66), channel_id=1, source_target_pairs={{0,8},{8,16},{16,24},{1,9},{9,17},{17,25},{2,10},{10,18},{18,26},{... | collective-permute-start | bytes 3896 | tf_op jit(solution)/shard_map/ppermute | solution.py:16
  48.2 2.3 collective-permute-start.4
  50.9 3.9 %collective-permute-start.2 = (f32[1,256,256]{2,1,0:T(8,128)S(1)}, f32[1,256,256]{2,1,0:T(8,128)S(1)}, u32[]{:S(2)}, u32[]{:S(2)}) collective-permute-start(f32[1,256,256]{2,1,0:T(8,128)S(1)} %convolution_bitcast_fusion.2), channel_id=1, source_target_pairs={{0,8},{8,16},{16,24},{1,9},{9,17},{17,25},{2,10},{10,18},{18,26},{... | collective-permute-start | bytes 786440 | tf_op jit(solution)/shard_map/ppermute | solution.py:16
  56.1 18.1 %copy.26 = f32[1,1,18,256,256]{2,4,3,1,0:T(8,128)} copy(f32[1,1,18,256,256]{4,3,2,1,0:T(8,128)} %param.11) | data formatting | bytes 9437184 | tf_op args[2]
  74.2 2.3 gather_fusion.1
  78.8 6.1 %fusion.8 = f32[256,18,256]{2,0,1:T(8,128)S(1)} fusion(f32[1,18,256,256]{3,2,1,0:T(8,128)} %param.10, f32[1,256,256]{2,1,0:T(8,128)S(1)} %collective-permute-done.2, pred[]{:T(512)S(6)} %eq.46), kind=kOutput, calls=%fused_computation.10 | convolution fusion | flops 3624075264 | bytes 9699329 | tf_op jit(solution)/shard_map/dot_general | solution.py:20
  84.9 4.0 %fusion.6 = f32[18,256,256]{2,1,0:T(8,128)S(1)} fusion(f32[256,18,256]{2,0,1:T(8,128)S(1)} %fusion.8, f32[1,256,256]{2,1,0:T(8,128)S(1)} %collective-permute-done.2, pred[]{:T(512)S(6)} %eq.46), kind=kOutput, calls=%fused_computation.8 | convolution fusion | flops 3624075264 | bytes 9699329 | tf_op jit(solution)/shard_map/dot_general | solution.py:20
  88.9 10.1 %fusion.14 = f32[18,256,256]{2,0,1:T(8,128)} fusion(f32[18,256,256]{2,1,0:T(8,128)S(1)} %fusion.6, f32[18,18]{1,0:T(8,128)S(1)} %collective-permute-done.5, pred[]{:T(512)S(6)} %eq.46), kind=kOutput, calls=%fused_computation.16 | convolution fusion | flops 254804944 | bytes 9438481 | tf_op jit(solution)/shard_map/vw,bvij->bwij/dot_general | solution.py:67
  99.1 17.6 %copy.29 = f32[18,256,256]{0,2,1:T(8,128)} copy(f32[18,256,256]{2,0,1:T(8,128)} %fusion.14) | data formatting | bytes 9437184 | tf_op jit(solution)/shard_map/squeeze | solution.py:20
  116.7 2.3 gather_fusion
  119.0 7.9 %fusion.12 = f32[18,256,256]{2,1,0:T(8,128)S(1)} fusion(f32[18,256,256]{2,0,1:T(8,128)} %fusion.14, f32[1,1,256,256]{3,2,1,0:T(8,128)S(1)} %copy-done.2, f32[]{:T(128)S(6)} %sqrt.9, f32[256]{0:T(256)S(1)} %get-tuple-element.16, f32[256]{0:T(256)S(1)} %get-tuple-element.17), kind=kOutput, calls=%fused_computation.14 | convolution fusion | flops 3624075264 | bytes 9701380 | tf_op jit(solution)/shard_map/dot_general | solution.py:20
  126.9 9.5 %fusion.28 = f32[256,256]{1,0:T(8,128)S(1)} fusion(f32[18,256,256]{2,1,0:T(8,128)S(1)} %fusion.12, f32[1,1,18,256,256]{4,3,2,1,0:T(8,128)} %param.11), kind=kOutput, calls=%fused_computation.31 | convolution fusion | flops 3623878656 | bytes 9699328 | tf_op jit(solution)/shard_map/dot_general | solution.py:20
  136.5 4.4 %fusion.19 = f32[1,256,256]{2,0,1:T(1,128)S(1)} fusion(f32[8,256,256]{2,1,0:T(8,128)} %bitcast.149, s32[]{:T(128)} %bitcast.26), kind=kOutput, calls=%fused_computation.19 | convolution fusion | flops 6291464 | bytes 2359300 | tf_op jit(solution)/shard_map/ji,ipc->jpc/dot_general | solution.py:88
  141.9 17.7 %psum.36 = f32[]{:T(128)} all-reduce(f32[]{:T(128)} %get-tuple-element.11), channel_id=1, replica_groups=mesh['seg'=4,'sec'=8] {'sec'}, use_global_device_ids=true, to_apply=%region_3.4 | all-reduce | flops 1 | bytes 8 | tf_op jit(solution)/shard_map/psum | solution.py:92
  161.4 20.0 %psum.37 = f32[]{:T(128)} all-reduce(f32[]{:T(128)} %get-tuple-element.7), channel_id=1, replica_groups=mesh['seg'=4,'sec'=8] {'sec'}, use_global_device_ids=true, to_apply=%region_5.6 | all-reduce | flops 1 | bytes 8 | tf_op jit(solution)/shard_map/psum | solution.py:28
  183.2 7.6 %fusion.10 = f32[18,256,256]{2,1,0:T(8,128)S(1)} fusion(f32[18,256,256]{2,0,1:T(8,128)} %fusion.14, f32[256,256]{1,0:T(8,128)S(1)} %get-tuple-element.8, f32[]{:T(128)S(6)} %sqrt.10), kind=kOutput, calls=%fused_computation.12 | convolution fusion | flops 3623944192 | bytes 9699332 | tf_op jit(solution)/shard_map/dot_general | solution.py:20
  190.9 4.1 %fusion.25 = f32[256,256]{1,0:T(8,128)S(1)} fusion(f32[18,256,256]{2,1,0:T(8,128)S(1)} %fusion.10, f32[1,1,18,256,256]{4,3,2,1,0:T(8,128)S(1)} %bitcast.147), kind=kOutput, calls=%fused_computation.30 | convolution fusion | flops 3623878656 | bytes 9699328 | tf_op jit(solution)/shard_map/dot_general | solution.py:20
  195.0 33.5 %all-gather.7.cloned.1.call-done = f32[2048,256]{1,0:T(8,128)} async-done(((f32[256,256]{1,0:T(8,128)}), f32[2048,256]{1,0:T(8,128)}) %all-gather.7.cloned.1.call-update) | async-done | bytes 2097168 | tf_op jit(solution)/shard_map/all_gather | solution.py:85
  228.5 4.3 %fusion.17 = f32[1,256,256]{2,0,1:T(1,128)S(1)} fusion(f32[8,256,256]{2,1,0:T(8,128)} %bitcast.150, s32[]{:T(128)} %bitcast.26), kind=kOutput, calls=%fused_computation.17 | convolution fusion | flops 6291464 | bytes 2359300 | tf_op jit(solution)/shard_map/ji,ipc->jpc/dot_general | solution.py:88
  233.9 19.5 %psum.38 = f32[]{:T(128)} all-reduce(f32[]{:T(128)} %get-tuple-element.14), channel_id=1, replica_groups=mesh['seg'=4,'sec'=8] {'sec'}, use_global_device_ids=true, to_apply=%region_7.8 | all-reduce | flops 1 | bytes 8 | tf_op jit(solution)/shard_map/psum | solution.py:92
  254.8 18.0 %psum.39 = f32[]{:T(128)} all-reduce(f32[]{:T(128)} %get-tuple-element.5), channel_id=1, replica_groups=mesh['seg'=4,'sec'=8] {'sec'}, use_global_device_ids=true, to_apply=%region_9.10 | all-reduce | flops 1 | bytes 8 | tf_op jit(solution)/shard_map/psum | solution.py:28
  (48 shorter events, 19.9 us)
Async XLA Ops:
  6.5 1.4 copy-start
  6.5 129.9 %all-gather.5.cloned.1.call-start = ((), (), s32[]{:S(2)}) async-start(), calls=%async_computation | async-start | bytes 2359296 | tf_op jit(solution)/shard_map/all_gather | solution.py:85
  11.3 28.4 %collective-permute-start = (f32[1,256,256]{2,1,0:T(8,128)S(1)}, f32[1,256,256]{2,1,0:T(8,128)S(1)}, u32[]{:S(2)}, u32[]{:S(2)}) collective-permute-start(f32[1,256,256]{2,1,0:T(8,128)S(1)} %convolution_bitcast_fusion.4), channel_id=1, source_target_pairs={{0,8},{8,16},{16,24},{1,9},{9,17},{17,25},{2,10},{10,18},{18,26},{... | collective-permute-start | bytes 786440 | tf_op jit(solution)/shard_map/ppermute | solution.py:16
  39.6 188.9 %all-gather.7.cloned.1.call-start = ((), (), s32[]{:S(2)}) async-start(), calls=%async_computation.1 | async-start | bytes 2359296 | tf_op jit(solution)/shard_map/all_gather | solution.py:85
  40.1 10.4 %collective-permute-start.1 = (f32[1,256,256]{2,1,0:T(8,128)S(1)}, f32[1,256,256]{2,1,0:T(8,128)S(1)}, u32[]{:S(2)}, u32[]{:S(2)}) collective-permute-start(f32[1,256,256]{2,1,0:T(8,128)S(1)} %convolution_bitcast_fusion.3), channel_id=1, source_target_pairs={{0,8},{8,16},{16,24},{1,9},{9,17},{17,25},{2,10},{10,18},{18,26},{... | collective-permute-start | bytes 786440 | tf_op jit(solution)/shard_map/ppermute | solution.py:16
  42.3 5.1 %collective-permute-start.3 = (f32[18,18]{1,0:T(8,128)S(1)}, f32[18,18]{1,0:T(8,128)S(1)}, u32[]{:S(2)}, u32[]{:S(2)}) collective-permute-start(f32[18,18]{1,0:T(8,128)S(1)} %fusion.66), channel_id=1, source_target_pairs={{0,8},{8,16},{16,24},{1,9},{9,17},{17,25},{2,10},{10,18},{18,26},{... | collective-permute-start | bytes 3896 | tf_op jit(solution)/shard_map/ppermute | solution.py:16
  48.2 28.3 %collective-permute-start.4 = (f32[18,18]{1,0:T(8,128)S(1)}, f32[18,18]{1,0:T(8,128)S(1)}, u32[]{:S(2)}, u32[]{:S(2)}) collective-permute-start(f32[18,18]{1,0:T(8,128)S(1)} %fusion.60), channel_id=1, source_target_pairs={{0,8},{8,16},{16,24},{1,9},{9,17},{17,25},{2,10},{10,18},{18,26},{... | collective-permute-start | bytes 3896 | tf_op jit(solution)/shard_map/ppermute | solution.py:16
  50.9 27.9 %collective-permute-start.2 = (f32[1,256,256]{2,1,0:T(8,128)S(1)}, f32[1,256,256]{2,1,0:T(8,128)S(1)}, u32[]{:S(2)}, u32[]{:S(2)}) collective-permute-start(f32[1,256,256]{2,1,0:T(8,128)S(1)} %convolution_bitcast_fusion.2), channel_id=1, source_target_pairs={{0,8},{8,16},{16,24},{1,9},{9,17},{17,25},{2,10},{10,18},{18,26},{... | collective-permute-start | bytes 786440 | tf_op jit(solution)/shard_map/ppermute | solution.py:16
  56.1 20.5 %copy-start.3 = (f32[1,18,18]{2,0,1:T(1,128)S(1)}, f32[1,18,18]{2,0,1:T(1,128)}, u32[]{:S(2)}) copy-start(f32[1,18,18]{2,0,1:T(1,128)} %param.13) | copy-start | bytes 3892
  76.7 12.2 %collective-permute-start.5 = (f32[18,18]{1,0:T(8,128)S(1)}, f32[18,18]{1,0:T(8,128)S(1)}, u32[]{:S(2)}, u32[]{:S(2)}) collective-permute-start(f32[18,18]{1,0:T(8,128)S(1)} %fusion.61), channel_id=1, source_target_pairs={{0,8},{8,16},{16,24},{1,9},{9,17},{17,25},{2,10},{10,18},{18,26},{... | collective-permute-start | bytes 3896 | tf_op jit(solution)/shard_map/ppermute | solution.py:16
  99.1 20.0 %copy-start.2 = (f32[1,1,256,256]{3,2,1,0:T(8,128)S(1)}, f32[1,1,256,256]{3,2,1,0:T(8,128)}, u32[]{:S(2)}) copy-start(f32[1,1,256,256]{3,2,1,0:T(8,128)} %param.9) | copy-start | bytes 786436
  126.9 14.0 %copy-start.5 = (f32[1,1,256,256]{3,2,1,0:T(8,128)S(1)}, f32[1,1,256,256]{3,2,1,0:T(8,128)}, u32[]{:S(2)}) copy-start(f32[1,1,256,256]{3,2,1,0:T(8,128)} %param.14) | copy-start | bytes 786436
  136.5 45.6 %copy-start.4 = (f32[1,1,256,256]{3,2,1,0:T(8,128)S(1)}, f32[1,1,256,256]{3,2,1,0:T(8,128)}, u32[]{:S(2)}) copy-start(f32[1,1,256,256]{3,2,1,0:T(8,128)} %param.15) | copy-start | bytes 786436
  159.6 31.2 %slice-start = ((s8[4718592]{0:T(1024)(128)(4,1)}), s8[524288]{0:T(1024)(128)(4,1)S(1)}, s32[]{:S(2)}) async-start(s8[4718592]{0:T(1024)(128)(4,1)} %bitcast.146), calls=%async_computation.2 | async-start | bytes 1048576
  183.2 7.7 %slice-start.1 = ((s8[4718592]{0:T(1024)(128)(4,1)}), s8[4194304]{0:T(1024)(128)(4,1)S(1)}, s32[]{:S(2)}) async-start(s8[4718592]{0:T(1024)(128)(4,1)} %bitcast.146), calls=%async_computation.3 | async-start | bytes 8388608
  190.9 83.3 %copy-start.1 = (f32[1,1,256,256]{3,2,1,0:T(8,128)S(1)}, f32[1,1,256,256]{3,2,1,0:T(8,128)}, u32[]{:S(2)}) copy-start(f32[1,1,256,256]{3,2,1,0:T(8,128)} %param.12) | copy-start | bytes 786436
Sparse Core Ops, SparseCore 0:
  39.8 46.7 all-gather.4
  183.3 45.1 all-gather.6
where the time goes:
time: 286 us; the launch traced here: 281 us
  blocking collectives  98.3 us (34%)
  matrix products  68 us (24%)
  local copies, waits for them, and re-layouts  43.1 us (15%)
  waiting for transfers between devices  34.4 us (12%)
  starting transfers between devices  16.2 us (6%)
  between operations  16.2 us (6%)
  other arithmetic  5.21 us (2%)
    psum x3, blocking collectives, norm_total(): return lax.psum(jnp.sum(vector * vector), 'sec')  61.1 us
    dot_general x16, matrix products, product(): return jnp.matmul(left, right, precision=HIGH)  47.4 us
    psum x2, blocking collectives, per_device(): rayleigh = lax.psum(jnp.sum(vector * image_vec), 'sec')  37.3 us
    all_gather x2, waiting for transfers between devices, per_device(): shard_piece = lax.all_gather(moving, 'sec', axis=0, tiled=True)  33.6 us
    unnamed x17, local copies, waits for them, and re-layouts  18.2 us
    squeeze x1, local copies, waits for them, and re-layouts, product(): return jnp.matmul(left, right, precision=HIGH)  17.6 us
    ppermute x6, starting transfers between devices, passed_along(): lax.ppermute(value, axis, [(source, source + steps) for source in range(i...  16.2 us
    dot_general x1, matrix products, per_device(): left_env = jnp.einsum('vw,bvij->bwij', prefix_mix, turned, precision=HIGH)  10.1 us
  transfers between devices with their start and end apart: 8, of which 2 were waited for; matrix products, arithmetic and copies ran while one was open for 34% of the time, Pallas kernels for 0%

commit v1 on v0

v1 whole, which is shorter than its diff:
```python
import functools
import math

import jax
import jax.numpy as jnp
from jax import lax
from jax.experimental import pallas as pl
from jax.experimental.pallas import tpu as pltpu
from jax.sharding import PartitionSpec as P

DAV = 2
EPSILON = 1e-06
HIGH = lax.Precision.HIGHEST
F32 = jnp.float32
BF16 = jnp.bfloat16
MESH = pl.DeviceIdType.MESH


def split(x):
    high = x.astype(BF16)
    return high, (x - high.astype(F32)).astype(BF16)


def left_cat(pair):
    high, low = pair
    return jnp.concatenate([high, high, low], axis=1)


def right_cat(pair):
    high, low = pair
    return jnp.concatenate([high, low, high], axis=0)


def dot(a, b):
    return jnp.dot(a, b, preferred_element_type=F32)


def exact(a, b, dims=((1,), (0,))):
    return lax.dot_general(a, b, (dims, ((), ())), precision=HIGH, preferred_element_type=F32)


def total(x):
    return jnp.sum(jnp.sum(x, axis=0, keepdims=True), axis=1, keepdims=True)


def octets(x):
    return jnp.sum(x.reshape(x.shape[0] // 8, 8, x.shape[1]), axis=0)


def kernel(
    nseg, nsec, W, N,
    sizes, sources, psi, boundary, right, own, mix, hop_left, hop_right,
    out,
    b_buf, r_buf, c_hi, c_lo, m_hi, m_lo, mixes, prefix, carry, diag_l, diag_r, diagonal, acc, vec,
    send_a, send_b, relay_a, relay_b, fwd_a, fwd_b, got_a, got_b,
    red0, red1, red2, red3, red4,
    load_sem, mix_send, mix_recv, chain_send, chain_recv,
    one_send, one_recv, two_send, two_recv, red_send, red_recv,
):
    seg, sec = lax.axis_index("seg"), lax.axis_index("sec")
    rows = N // nsec
    W8 = W * 8
    WP = mixes.shape[1]
    wide = -(-W // 8) * 8
    reds = (red0, red1, red2, red3, red4)
    sends, relays, fwds, gots = (send_a, send_b), (relay_a, relay_b), (fwd_a, fwd_b), (got_a, got_b)

    load_r = pltpu.make_async_copy(right, r_buf, load_sem.at[0])
    load_b = pltpu.make_async_copy(boundary, b_buf, load_sem.at[1])
    load_r.start()
    load_b.start()

    def other(index, step, count):
        return lax.rem(index + step, count)

    barrier = pltpu.get_barrier_semaphore()
    mixes[...] = jnp.zeros_like(mixes)
    mixes.at[seg][0:W, 0:W] = mix[...]
    for k in range(1, nsec):
        pl.semaphore_signal(barrier, inc=1, device_id={"sec": other(sec, k, nsec)}, device_id_type=MESH)
    for k in range(1, nseg):
        pl.semaphore_signal(barrier, inc=1, device_id={"seg": other(seg, k, nseg)}, device_id_type=MESH)

    @pl.when(seg == 0)
    def _():
        carry[...] = own[...]
        prefix[...] = jnp.where(
            lax.broadcasted_iota(jnp.int32, (N, N), 0) == lax.broadcasted_iota(jnp.int32, (N, N), 1), 1.0, 0.0
        )

    pl.semaphore_wait(barrier, nsec + nseg - 2)

    def mix_copy(k, slot):
        return pltpu.make_async_remote_copy(
            mixes.at[slot, pl.ds(0, wide)], mixes.at[slot, pl.ds(0, wide)],
            mix_send.at[k], mix_recv.at[k], device_id={"seg": other(seg, k, nseg)}, device_id_type=MESH,
        )

    for k in range(1, nseg):
        mix_copy(k, seg).start()

    halves = 2
    part = N // halves

    def chain_copy(i):
        return pltpu.make_async_remote_copy(
            carry.at[pl.ds(i * part, part)], prefix.at[pl.ds(i * part, part)],
            chain_send.at[i], chain_recv.at[i],
            device_id={"seg": lax.rem(seg + 1, nseg)}, device_id_type=MESH,
        )

    @pl.when(seg == 0)
    def _():
        for i in range(halves):
            chain_copy(i).start()

    def chain_step():
        for i in range(halves):
            chain_copy(i).wait_recv()

            @pl.when(seg < nseg - 1)
            def _():
                here = pl.ds(i * part, part)
                carry[here] = exact(prefix[here], own[...])
                chain_copy(i).start()

    def reduce_copy(r, k, slot):
        return pltpu.make_async_remote_copy(
            reds[r].at[slot], reds[r].at[slot], red_send.at[r, k], red_recv.at[r, k],
            device_id={"sec": other(sec, k, nsec)}, device_id_type=MESH,
        )

    def reduce_start(r, value):
        reds[r].at[sec][...] = jnp.broadcast_to(value, (8, 128))
        for k in range(1, nsec):
            reduce_copy(r, k, sec).start()

    def reduce_end(r):
        for k in range(1, nsec):
            reduce_copy(r, k, lax.rem(sec + nsec - k, nsec)).wait_recv()
        return jnp.sum(reds[r][...], axis=0)[0:1, 0:1]

    def one_copy(t, k, piece, slot):
        return pltpu.make_async_remote_copy(
            sends[t].at[piece], relays[t].at[slot], one_send.at[t, k], one_recv.at[t, k],
            device_id={"sec": other(sec, k, nsec)}, device_id_type=MESH,
        )

    def two_copy(t, k, piece, slot):
        return pltpu.make_async_remote_copy(
            fwds[t].at[piece], gots[t].at[slot], two_send.at[t, k], two_recv.at[t, k],
            device_id={"sec": other(sec, k, nsec)}, device_id_type=MESH,
        )

    def permute_start(t, value):
        sends[t][...] = value.reshape(nsec, rows, N)
        for k in range(1, nsec):
            one_copy(t, k, other(sec, k, nsec), sec).start()
        relays[t].at[sec][...] = sends[t].at[sec][...]

    def permute_turn(t):
        for k in range(1, nsec):
            one_copy(t, k, sec, lax.rem(sec + nsec - k, nsec)).wait_recv()
        for d in range(nsec):
            fwds[t][d] = relays[t][sources[0, d]]
        for k in range(1, nsec):
            two_copy(t, k, other(sec, k, nsec), sec).start()
        gots[t].at[sec][...] = fwds[t].at[sec][...]

    def permute_end(t):
        for k in range(1, nsec):
            two_copy(t, k, sec, lax.rem(sec + nsec - k, nsec)).wait_recv()
        return gots[t][...].reshape(N, N)

    places_i = lax.broadcasted_iota(jnp.int32, (N, N), 0)
    places_j = lax.broadcasted_iota(jnp.int32, (N, N), 1)

    def masked(x):
        return jnp.where((places_i < sizes[0, sec]) & (places_j < sizes[1, sec]), x, 0.0)

    hop_right_cat = right_cat(split(hop_right[...]))
    start = masked(psi[...])
    permute_start(0, dot(left_cat(split(start)), hop_right_cat))
    reduce_start(0, total(start * start))

    @pl.when((seg > 0) & (seg < 2))
    def _():
        chain_step()

    for k in range(1, nseg):
        mix_copy(k, lax.rem(seg + nseg - k, nseg)).wait_recv()
    prefix_mix = jnp.where(
        lax.broadcasted_iota(jnp.int32, (WP, WP), 0) == lax.broadcasted_iota(jnp.int32, (WP, WP), 1), 1.0, 0.0
    )
    for t in range(nseg - 1):
        prefix_mix = jnp.where(t < seg, exact(prefix_mix, mixes[t]), prefix_mix)
    spread = jnp.where(
        lax.broadcasted_iota(jnp.int32, (W8, WP), 0) // 8 == lax.broadcasted_iota(jnp.int32, (W8, WP), 1), 1.0, 0.0
    )
    mix_full = exact(exact(spread, prefix_mix), spread, ((1,), (1,)))
    same = (
        lax.broadcasted_iota(jnp.int32, (W8, W8), 0) % 8 == lax.broadcasted_iota(jnp.int32, (W8, W8), 1) % 8
    )
    k_hi, k_lo = split(jnp.where(same, mix_full, 0.0))
    load_r.wait()

    @pl.loop(0, N // 16)
    def _(c):
        here = pl.ds(pl.multiple_of(c * 16, 16), 16)
        chunk = r_buf[:, here, :]
        side = jnp.concatenate([chunk[:, 0:8].reshape(W8, N), chunk[:, 8:16].reshape(W8, N)], axis=1)
        s_hi, s_lo = split(side)
        mixed = dot(k_hi, s_hi) + (dot(k_hi, s_lo) + dot(k_lo, s_hi))
        mixed = jnp.concatenate([mixed[:, :N].reshape(W, 8, N), mixed[:, N:].reshape(W, 8, N)], axis=1)
        o_hi, o_lo = split(mixed)
        m_hi[:, here, :] = o_hi
        m_lo[:, here, :] = o_lo

    @pl.loop(0, W)
    def _(w):
        diag_r.at[w][...] = octets(jnp.where(places_i == places_j, r_buf.at[w][...], 0.0))

    permute_turn(0)

    @pl.when(seg >= 2)
    def _():
        chain_step()

    pre = prefix[...]
    pre_turned = left_cat(split(pre.T))
    load_b.wait()

    @pl.loop(0, W)
    def _(w):
        moved = exact(b_buf.at[w][...], prefix[...])
        diag_l.at[w][...] = octets(prefix[...] * moved)
        high, low = split(moved)
        c_hi.at[w][...] = high
        c_lo.at[w][...] = low

    side_r = exact(mix_full, diag_r[...].reshape(W8, N))
    diagonal[...] = exact(diag_l[...].reshape(W8, N), side_r, ((0,), (0,)))

    hop_left_cat = left_cat(split(hop_left[...]))
    group = 3 if W % 3 == 0 else 1

    def local_part(x_cat, first, last):
        @pl.loop(first, last)
        def _(g):
            base = g * group
            for i in range(group):
                w = base + i
                y = dot(left_cat((c_hi.at[w][...], c_lo.at[w][...])), x_cat)
                acc[...] += dot(left_cat(split(y)), right_cat((m_hi.at[w][...], m_lo.at[w][...])))

    steps = W // group
    norm = jnp.sqrt(reduce_end(0) + EPSILON)
    vec[...] = masked(psi[...]) / norm
    hop_scale = 1.0 / norm
    for t in range(DAV):
        x_cat = right_cat(split(vec[...]))
        acc[...] = jnp.zeros_like(acc)
        if t == 0:
            local_part(x_cat, 0, steps)
        else:
            local_part(x_cat, 0, steps // 2)
            permute_turn(t)
            local_part(x_cat, steps // 2, steps)
            norm = jnp.sqrt(reduce_end(2) + EPSILON)
            own_scale = own_norm / norm
            hop_scale = jnp.sqrt(reds[2][sources[0, sec]][0:1, 0:1] + EPSILON) / norm
        local = dot(pre_turned, right_cat(split(acc[...])))
        if t > 0:
            local = local * own_scale
            vec[...] = vec[...] * own_scale
        hop = dot(hop_left_cat, right_cat(split(permute_end(t))))
        image = masked(local + hop * hop_scale)
        vector = vec[...]
        reduce_start(2 * t + 1, total(vector * image))
        acc[...] = image
        rayleigh = reduce_end(2 * t + 1)
        vector = vec[...]
        residue = acc[...] - rayleigh * vector
        shifted = diagonal[...] - rayleigh
        update = vector - residue * shifted / (shifted * shifted + 1.0)
        squares = total(update * update)
        reduce_start(2 * t + 2, squares)
        if t < DAV - 1:
            own_norm = jnp.sqrt(squares + EPSILON)
            scaled = update / own_norm
            vec[...] = scaled
            permute_start(t + 1, dot(left_cat(split(scaled)), hop_right_cat))
        else:
            acc[...] = update
    norm = jnp.sqrt(reduce_end(2 * DAV) + EPSILON)
    out[...] = acc[...] * (math.sqrt(float(nsec * N * N)) / norm)

    for k in range(1, nseg):
        mix_copy(k, seg).wait_send()

    @pl.when(seg < nseg - 1)
    def _():
        for i in range(halves):
            chain_copy(i).wait_send()

    for k in range(1, nsec):
        for r in range(5):
            reduce_copy(r, k, sec).wait_send()
        for t in range(DAV):
            one_copy(t, k, other(sec, k, nsec), sec).wait_send()
            two_copy(t, k, other(sec, k, nsec), sec).wait_send()


def per_device(
    nseg, nsec,
    psi_init, boundary_env, right_env, transfer_blocks, transfer_mix, hop_left, hop_right, block_sizes, sources,
):
    W, N = right_env.shape[2], right_env.shape[3]
    rows = N // nsec
    WP = 128
    vmem = pl.BlockSpec(memory_space=pltpu.VMEM)
    smem = pl.BlockSpec(memory_space=pltpu.SMEM)
    hbm = pl.BlockSpec(memory_space=pl.ANY)
    square = pltpu.VMEM((N, N), F32)
    pieces = pltpu.VMEM((nsec, rows, N), F32)
    result = pl.pallas_call(
        functools.partial(kernel, nseg, nsec, W, N),
        out_shape=jax.ShapeDtypeStruct((N, N), F32),
        in_specs=[smem, smem, vmem, hbm, hbm, vmem, vmem, vmem, vmem],
        out_specs=vmem,
        scratch_shapes=[
            pltpu.VMEM((W, N, N), F32),
            pltpu.VMEM((W, N, N), F32),
            pltpu.VMEM((W, N, N), BF16),
            pltpu.VMEM((W, N, N), BF16),
            pltpu.VMEM((W, N, N), BF16),
            pltpu.VMEM((W, N, N), BF16),
            pltpu.VMEM((nseg, WP, WP), F32),
            square,
            square,
            pltpu.VMEM((W, 8, N), F32),
            pltpu.VMEM((W, 8, N), F32),
            square,
            square,
            square,
        ]
        + [pieces] * 8
        + [pltpu.VMEM((nsec, 8, 128), F32)] * 5
        + [
            pltpu.SemaphoreType.DMA((2,)),
            pltpu.SemaphoreType.DMA((nseg,)),
            pltpu.SemaphoreType.DMA((nseg,)),
            pltpu.SemaphoreType.DMA((2,)),
            pltpu.SemaphoreType.DMA((2,)),
            pltpu.SemaphoreType.DMA((2, nsec)),
            pltpu.SemaphoreType.DMA((2, nsec)),
            pltpu.SemaphoreType.DMA((2, nsec)),
            pltpu.SemaphoreType.DMA((2, nsec)),
            pltpu.SemaphoreType.DMA((5, nsec)),
            pltpu.SemaphoreType.DMA((5, nsec)),
        ],
        compiler_params=pltpu.CompilerParams(
            collective_id=0, has_side_effects=True, vmem_limit_bytes=48 * 1024 * 1024
        ),
    )(
        block_sizes[0], sources, psi_init[0, 0], boundary_env[0], right_env[0, 0], transfer_blocks[0, 0],
        transfer_mix[0], hop_left[0, 0], hop_right[0, 0],
    )
    return result[None, None]


def solution(mesh):
    return jax.shard_map(
        functools.partial(per_device, mesh.shape["seg"], mesh.shape["sec"]),
        mesh=mesh,
        in_specs=(
            P("seg", "sec", None, None),
            P("sec", None, None, None),
            P("seg", "sec", None, None, None),
            P("seg", "sec", None, None),
            P("seg", None, None),
            P("seg", "sec", None, None),
            P("seg", "sec", None, None),
            P("seg", None, None),
            P("seg", None),
        ),
        out_specs=P("seg", "sec", None, None),
        check_vma=False,
    )
```

time: 286 us -> 68 us (0.24); the launches traced: 281 us -> 67.6 us
  blocking collectives: 98.3 us -> 0 us
  matrix products: 68 us -> 0 us
  Pallas kernels: 0 us -> 58.7 us
  waiting for transfers between devices: 34.4 us -> 0 us
  local copies, waits for them, and re-layouts: 43.1 us -> 8.87 us
  starting transfers between devices: 16.2 us -> 0 us
  between operations: 16.2 us -> 0.02 us
  other arithmetic: 5.21 us -> 0 us
    psum x5 -> x0, blocking collectives: 98.3 us -> none  [the longest x3 61.1 us: norm_total(): return lax.psum(jnp.sum(vector * vector), 'sec')]
    dot_general x20 -> x0, matrix products: 68 us -> none  [the longest x16 47.4 us: product(): return jnp.matmul(left, right, precision=HIGH)]
    pallas_call x0 -> x1, Pallas kernels: none -> 58.7 us  [per_device(): pl.pallas_call(functools.partial(kernel, nseg, nsec, W, N), out_shape=jax...]
    all_gather x2 -> x0, waiting for transfers between devices: 33.6 us -> none  [per_device(): shard_piece = lax.all_gather(moving, 'sec', axis=0, tiled=True)]
    squeeze x1 -> x0, local copies, waits for them, and re-layouts: 17.6 us -> none  [product(): return jnp.matmul(left, right, precision=HIGH)]
    ppermute x6 -> x0, starting transfers between devices: 16.2 us -> none  [passed_along(): lax.ppermute(value, axis, [(source, source + steps) for source in range(i...]
    unnamed x17 -> x16, local copies, waits for them, and re-layouts: 18.2 us -> 8.87 us
    gather x2 -> x0, local copies, waits for them, and re-layouts: 4.66 us -> none  [the longest x1 2.34 us: per_device(): jnp.diagonal(right_side, axis1=2, axis2=3)]
  transfers between devices with their start and end apart: 8 -> 0, of which waited for: 2 -> 0; matrix products, arithmetic and copies ran while one was open for 34% -> 0% of each run, Pallas kernels for 0% -> 0%
where the time goes in v1:
time: 68 us; the launch traced here: 67.6 us
  Pallas kernels  58.7 us (86%)
  local copies, waits for them, and re-layouts  8.87 us (13%)
    pallas_call x1, Pallas kernels, per_device(): pl.pallas_call(functools.partial(kernel, nseg, nsec, W, N), out_shape=jax...  58.7 us
    unnamed x16, local copies, waits for them, and re-layouts  8.87 us

profile of v1, /device:TPU:0, one launch (start us, length us, event | category | flops | bytes accessed | tf_op | source)
XLA Modules:
  0.0 67.6 jit_solution(624342403530285296)
XLA Ops:
  0.0 0.7 %copy.12 = f32[1,18,18]{2,1,0:T(8,128)S(1)} copy(f32[1,18,18]{2,0,1:T(1,128)} %param.13) | data formatting | bytes 2592
  0.7 0.0 copy-start
  0.7 2.3 %copy-done = f32[1,18,256,256]{3,2,1,0:T(8,128)S(1)} copy-done((f32[1,18,256,256]{3,2,1,0:T(8,128)S(1)}, f32[1,18,256,256]{3,2,1,0:T(8,128)}, u32[]{:S(2)}) %copy-start) | copy-done | bytes 4718616
  3.0 0.0 copy-start.1
  3.0 0.9 %copy-done.1 = f32[1,1,256,256]{3,2,1,0:T(8,128)S(1)} copy-done((f32[1,1,256,256]{3,2,1,0:T(8,128)S(1)}, f32[1,1,256,256]{3,2,1,0:T(8,128)}, u32[]{:S(2)}) %copy-start.1) | copy-done | bytes 262168
  4.0 0.0 copy-start.2
  4.0 0.9 %copy-done.2 = f32[1,1,256,256]{3,2,1,0:T(8,128)S(1)} copy-done((f32[1,1,256,256]{3,2,1,0:T(8,128)S(1)}, f32[1,1,256,256]{3,2,1,0:T(8,128)}, u32[]{:S(2)}) %copy-start.2) | copy-done | bytes 262168
  4.9 0.0 copy-start.3
  4.9 0.9 %copy-done.3 = f32[1,1,256,256]{3,2,1,0:T(8,128)S(1)} copy-done((f32[1,1,256,256]{3,2,1,0:T(8,128)S(1)}, f32[1,1,256,256]{3,2,1,0:T(8,128)}, u32[]{:S(2)}) %copy-start.3) | copy-done | bytes 262168
  5.9 0.0 copy-start.4
  5.9 0.9 %copy-done.4 = f32[1,1,256,256]{3,2,1,0:T(8,128)S(1)} copy-done((f32[1,1,256,256]{3,2,1,0:T(8,128)S(1)}, f32[1,1,256,256]{3,2,1,0:T(8,128)}, u32[]{:S(2)}) %copy-start.4) | copy-done | bytes 262168
  6.8 0.0 copy-start.5
  6.8 0.7 %copy-done.5 = s32[1,2,8]{2,1,0:T(2,128)S(1)} copy-done((s32[1,2,8]{2,1,0:T(2,128)S(1)}, s32[1,2,8]{2,1,0:T(2,128)}, u32[]{:S(2)}) %copy-start.5) | copy-done | bytes 88
  7.5 0.0 copy-start.6
  7.5 0.7 copy-done.6
  8.2 58.7 %shard_map.91 = f32[256,256]{1,0:T(8,128)S(1)} custom-call(s32[2,8]{1,0:T(2,128)S(1)} %bitcast.18, s32[1,8]{1,0:T(1,128)S(1)} %copy-done.6, f32[256,256]{1,0:T(8,128)S(1)} %bitcast.13, f32[18,256,256]{2,1,0:T(8,128)S(1)} %bitcast.11, f32[18,256,256]{2,1,0:T(8,128)} %bitcast.19, f32[256,256]{1,0:T(8,128)S(1)} %bitcast.14, f32[18,18]{1,0:T(8,128)S(1)} %bitcast.17, ...), custom_call_target="tpu_custom_call" | custom-call | tf_op jit(solution)/shard_map/pallas_call | solution.py:326
  66.9 0.7 %copy.14 = f32[1,1,256,256]{3,2,1,0:T(8,128)} copy(f32[1,1,256,256]{3,2,1,0:T(8,128)S(1)} %bitcast.12) | data formatting | bytes 524288
Async XLA Ops:
  0.7 2.3 %copy-start = (f32[1,18,256,256]{3,2,1,0:T(8,128)S(1)}, f32[1,18,256,256]{3,2,1,0:T(8,128)}, u32[]{:S(2)}) copy-start(f32[1,18,256,256]{3,2,1,0:T(8,128)} %param.10) | copy-start | bytes 14155780
  3.0 0.9 %copy-start.1 = (f32[1,1,256,256]{3,2,1,0:T(8,128)S(1)}, f32[1,1,256,256]{3,2,1,0:T(8,128)}, u32[]{:S(2)}) copy-start(f32[1,1,256,256]{3,2,1,0:T(8,128)} %param.9) | copy-start | bytes 786436
  4.0 0.9 %copy-start.2 = (f32[1,1,256,256]{3,2,1,0:T(8,128)S(1)}, f32[1,1,256,256]{3,2,1,0:T(8,128)}, u32[]{:S(2)}) copy-start(f32[1,1,256,256]{3,2,1,0:T(8,128)} %param.12) | copy-start | bytes 786436
  4.9 0.9 %copy-start.3 = (f32[1,1,256,256]{3,2,1,0:T(8,128)S(1)}, f32[1,1,256,256]{3,2,1,0:T(8,128)}, u32[]{:S(2)}) copy-start(f32[1,1,256,256]{3,2,1,0:T(8,128)} %param.14) | copy-start | bytes 786436
  5.9 0.9 %copy-start.4 = (f32[1,1,256,256]{3,2,1,0:T(8,128)S(1)}, f32[1,1,256,256]{3,2,1,0:T(8,128)}, u32[]{:S(2)}) copy-start(f32[1,1,256,256]{3,2,1,0:T(8,128)} %param.15) | copy-start | bytes 786436
  6.8 0.7 %copy-start.5 = (s32[1,2,8]{2,1,0:T(2,128)S(1)}, s32[1,2,8]{2,1,0:T(2,128)}, u32[]{:S(2)}) copy-start(s32[1,2,8]{2,1,0:T(2,128)} %param.16) | copy-start | bytes 196
  7.5 0.7 copy-start.6

commit v2 on v1

--- a/solution.py
+++ b/solution.py
@@ -49,8 +49,9 @@
 
 def kernel(
     nseg, nsec, W, N,
-    sizes, sources, psi, boundary, right, own, mix, hop_left, hop_right,
+    sizes, sources, psi_in, boundary, right, own_in, mix_in, hop_left_in, hop_right_in,
     out,
+    psi, own, mix, hop_left, hop_right,
     b_buf, r_buf, c_hi, c_lo, m_hi, m_lo, mixes, prefix, carry, diag_l, diag_r, diagonal, acc, vec,
     send_a, send_b, relay_a, relay_b, fwd_a, fwd_b, got_a, got_b,
     red0, red1, red2, red3, red4,
@@ -67,6 +68,14 @@
 
     load_r = pltpu.make_async_copy(right, r_buf, load_sem.at[0])
     load_b = pltpu.make_async_copy(boundary, b_buf, load_sem.at[1])
+    loads = [
+        pltpu.make_async_copy(source, target, load_sem.at[2 + i])
+        for i, (source, target) in enumerate(
+            [(mix_in, mix), (own_in, own), (psi_in, psi), (hop_right_in, hop_right), (hop_left_in, hop_left)]
+        )
+    ]
+    for load in loads:
+        load.start()
     load_r.start()
     load_b.start()
 
@@ -75,11 +84,14 @@
 
     barrier = pltpu.get_barrier_semaphore()
     mixes[...] = jnp.zeros_like(mixes)
-    mixes.at[seg][0:W, 0:W] = mix[...]
     for k in range(1, nsec):
         pl.semaphore_signal(barrier, inc=1, device_id={"sec": other(sec, k, nsec)}, device_id_type=MESH)
     for k in range(1, nseg):
         pl.semaphore_signal(barrier, inc=1, device_id={"seg": other(seg, k, nseg)}, device_id_type=MESH)
+
+    loads[0].wait()
+    mixes.at[seg][0:W, 0:W] = mix[...]
+    loads[1].wait()
 
     @pl.when(seg == 0)
     def _():
@@ -178,6 +190,8 @@
     def masked(x):
         return jnp.where((places_i < sizes[0, sec]) & (places_j < sizes[1, sec]), x, 0.0)
 
+    loads[2].wait()
+    loads[3].wait()
     hop_right_cat = right_cat(split(hop_right[...]))
     start = masked(psi[...])
     permute_start(0, dot(left_cat(split(start)), hop_right_cat))
@@ -227,12 +241,16 @@
         chain_step()
 
     pre = prefix[...]
+    p_hi, p_lo = split(pre)
+    p_rest = (pre - p_hi.astype(F32) - p_lo.astype(F32)).astype(BF16)
+    pre_cat = jnp.concatenate([p_hi, p_lo, p_rest, p_hi], axis=0)
     pre_turned = left_cat(split(pre.T))
     load_b.wait()
 
     @pl.loop(0, W)
     def _(w):
-        moved = exact(b_buf.at[w][...], prefix[...])
+        e_hi, e_lo = split(b_buf.at[w][...])
+        moved = dot(jnp.concatenate([e_hi, e_hi, e_hi, e_lo], axis=1), pre_cat)
         diag_l.at[w][...] = octets(prefix[...] * moved)
         high, low = split(moved)
         c_hi.at[w][...] = high
@@ -241,6 +259,7 @@
     side_r = exact(mix_full, diag_r[...].reshape(W8, N))
     diagonal[...] = exact(diag_l[...].reshape(W8, N), side_r, ((0,), (0,)))
 
+    loads[4].wait()
     hop_left_cat = left_cat(split(hop_left[...]))
     group = 3 if W % 3 == 0 else 1
 
@@ -320,15 +339,20 @@
     WP = 128
     vmem = pl.BlockSpec(memory_space=pltpu.VMEM)
     smem = pl.BlockSpec(memory_space=pltpu.SMEM)
-    hbm = pl.BlockSpec(memory_space=pl.ANY)
+    hbm = pl.BlockSpec(memory_space=pltpu.HBM)
     square = pltpu.VMEM((N, N), F32)
     pieces = pltpu.VMEM((nsec, rows, N), F32)
     result = pl.pallas_call(
         functools.partial(kernel, nseg, nsec, W, N),
         out_shape=jax.ShapeDtypeStruct((N, N), F32),
-        in_specs=[smem, smem, vmem, hbm, hbm, vmem, vmem, vmem, vmem],
+        in_specs=[smem, smem] + [hbm] * 7,
         out_specs=vmem,
         scratch_shapes=[
+            square,
+            square,
+            pltpu.VMEM((W, W), F32),
+            square,
+            square,
             pltpu.VMEM((W, N, N), F32),
             pltpu.VMEM((W, N, N), F32),
             pltpu.VMEM((W, N, N), BF16),
@@ -347,7 +371,7 @@
         + [pieces] * 8
         + [pltpu.VMEM((nsec, 8, 128), F32)] * 5
         + [
-            pltpu.SemaphoreType.DMA((2,)),
+            pltpu.SemaphoreType.DMA((7,)),
             pltpu.SemaphoreType.DMA((nseg,)),
             pltpu.SemaphoreType.DMA((nseg,)),
             pltpu.SemaphoreType.DMA((2,)),
@@ -360,7 +384,7 @@
             pltpu.SemaphoreType.DMA((5, nsec)),
         ],
         compiler_params=pltpu.CompilerParams(
-            collective_id=0, has_side_effects=True, vmem_limit_bytes=48 * 1024 * 1024
+            collective_id=0, has_side_effects=True, vmem_limit_bytes=(65536 - 320) * 1024
         ),
     )(
         block_sizes[0], sources, psi_init[0, 0], boundary_env[0], right_env[0, 0], transfer_blocks[0, 0],

time: 68 us -> 61.6 us (0.906)
  local copies, waits for them, and re-layouts: 8.87 us -> 2.97 us
    unnamed x16 -> x2, local copies, waits for them, and re-layouts: 8.87 us -> 2.97 us
where the time goes in v2:
time: 61.6 us; the launch traced here: 61.3 us
  Pallas kernels  58.3 us (95%)
  local copies, waits for them, and re-layouts  2.97 us (5%)
    pallas_call x1, Pallas kernels, per_device(): pl.pallas_call(functools.partial(kernel, nseg, nsec, W, N), out_shape=jax...  58.3 us
    unnamed x2, local copies, waits for them, and re-layouts  2.97 us

profile of v2, /device:TPU:0, one launch (start us, length us, event | category | flops | bytes accessed | tf_op | source)
XLA Modules:
  0.0 61.3 jit_solution(3219028977600836518)
XLA Ops:
  0.0 1.3 %copy.12 = f32[1,18,18]{2,1,0:T(8,128)} copy(f32[1,18,18]{2,0,1:T(1,128)} %param.13) | data formatting | bytes 2592
  1.3 58.3 %shard_map.91 = f32[256,256]{1,0:T(8,128)} custom-call(s32[2,8]{1,0:T(2,128)} %bitcast.19, s32[1,8]{1,0:T(1,128)} %sources.1, f32[256,256]{1,0:T(8,128)} %bitcast.14, f32[18,256,256]{2,1,0:T(8,128)} %bitcast.11, f32[18,256,256]{2,1,0:T(8,128)} %bitcast.12, f32[256,256]{1,0:T(8,128)} %bitcast.15, f32[18,18]{1,0:T(8,128)} %bitcast.18, f32[256,256]{1,0:T(8,128)} %bitcast.16, ...), custom_call_target="tpu_custom_call" | custom-call | tf_op jit(solution)/shard_map/pallas_call | solution.py:345
  59.6 1.7 %copy.14 = f32[1,1,256,256]{3,2,1,0:T(8,128)} copy(f32[1,1,256,256]{3,2,1,0:T(8,128)} %bitcast.13) | data formatting | bytes 524288

commit v3 on v2

--- a/solution.py
+++ b/solution.py
@@ -100,6 +100,18 @@
             lax.broadcasted_iota(jnp.int32, (N, N), 0) == lax.broadcasted_iota(jnp.int32, (N, N), 1), 1.0, 0.0
         )
 
+    places_i = lax.broadcasted_iota(jnp.int32, (N, N), 0)
+    places_j = lax.broadcasted_iota(jnp.int32, (N, N), 1)
+
+    def masked(x):
+        return jnp.where((places_i < sizes[0, sec]) & (places_j < sizes[1, sec]), x, 0.0)
+
+    loads[2].wait()
+    loads[3].wait()
+    hop_right_cat = right_cat(split(hop_right[...]))
+    start = masked(psi[...])
+    first_moving = dot(left_cat(split(start)), hop_right_cat)
+    first_squares = total(start * start)
     pl.semaphore_wait(barrier, nsec + nseg - 2)
 
     def mix_copy(k, slot):
@@ -184,18 +196,9 @@
             two_copy(t, k, sec, lax.rem(sec + nsec - k, nsec)).wait_recv()
         return gots[t][...].reshape(N, N)
 
-    places_i = lax.broadcasted_iota(jnp.int32, (N, N), 0)
-    places_j = lax.broadcasted_iota(jnp.int32, (N, N), 1)
-
-    def masked(x):
-        return jnp.where((places_i < sizes[0, sec]) & (places_j < sizes[1, sec]), x, 0.0)
-
-    loads[2].wait()
-    loads[3].wait()
-    hop_right_cat = right_cat(split(hop_right[...]))
-    start = masked(psi[...])
-    permute_start(0, dot(left_cat(split(start)), hop_right_cat))
-    reduce_start(0, total(start * start))
+
+    permute_start(0, first_moving)
+    reduce_start(0, first_squares)
 
     @pl.when((seg > 0) & (seg < 2))
     def _():
@@ -234,8 +237,6 @@
     def _(w):
         diag_r.at[w][...] = octets(jnp.where(places_i == places_j, r_buf.at[w][...], 0.0))
 
-    permute_turn(0)
-
     @pl.when(seg >= 2)
     def _():
         chain_step()
@@ -247,14 +248,19 @@
     pre_turned = left_cat(split(pre.T))
     load_b.wait()
 
-    @pl.loop(0, W)
-    def _(w):
-        e_hi, e_lo = split(b_buf.at[w][...])
-        moved = dot(jnp.concatenate([e_hi, e_hi, e_hi, e_lo], axis=1), pre_cat)
-        diag_l.at[w][...] = octets(prefix[...] * moved)
-        high, low = split(moved)
-        c_hi.at[w][...] = high
-        c_lo.at[w][...] = low
+    def left_part(first, last):
+        @pl.loop(first, last)
+        def _(w):
+            e_hi, e_lo = split(b_buf.at[w][...])
+            moved = dot(jnp.concatenate([e_hi, e_hi, e_hi, e_lo], axis=1), pre_cat)
+            diag_l.at[w][...] = octets(prefix[...] * moved)
+            high, low = split(moved)
+            c_hi.at[w][...] = high
+            c_lo.at[w][...] = low
+
+    left_part(0, W // 2)
+    permute_turn(0)
+    left_part(W // 2, W)
 
     side_r = exact(mix_full, diag_r[...].reshape(W8, N))
     diagonal[...] = exact(diag_l[...].reshape(W8, N), side_r, ((0,), (0,)))

time: 61.6 us -> 61.4 us (level)
  no operation moved by 1% of the time
where the time goes in v3:
time: 61.4 us; the launch traced here: 61.1 us
  Pallas kernels  58.2 us (95%)
  local copies, waits for them, and re-layouts  2.97 us (5%)
    pallas_call x1, Pallas kernels, per_device(): pl.pallas_call(functools.partial(kernel, nseg, nsec, W, N), out_shape=jax...  58.2 us
    unnamed x2, local copies, waits for them, and re-layouts  2.97 us

profile of v3, /device:TPU:0, one launch (start us, length us, event | category | flops | bytes accessed | tf_op | source)
XLA Modules:
  0.0 61.1 jit_solution(16310698289360865448)
XLA Ops:
  0.0 1.3 %copy.12 = f32[1,18,18]{2,1,0:T(8,128)} copy(f32[1,18,18]{2,0,1:T(1,128)} %param.13) | data formatting | bytes 2592
  1.3 58.2 %shard_map.91 = f32[256,256]{1,0:T(8,128)} custom-call(s32[2,8]{1,0:T(2,128)} %bitcast.19, s32[1,8]{1,0:T(1,128)} %sources.1, f32[256,256]{1,0:T(8,128)} %bitcast.14, f32[18,256,256]{2,1,0:T(8,128)} %bitcast.11, f32[18,256,256]{2,1,0:T(8,128)} %bitcast.12, f32[256,256]{1,0:T(8,128)} %bitcast.15, f32[18,18]{1,0:T(8,128)} %bitcast.18, f32[256,256]{1,0:T(8,128)} %bitcast.16, ...), custom_call_target="tpu_custom_call" | custom-call | tf_op jit(solution)/shard_map/pallas_call | solution.py:351
  59.5 1.7 %copy.14 = f32[1,1,256,256]{3,2,1,0:T(8,128)} copy(f32[1,1,256,256]{3,2,1,0:T(8,128)} %bitcast.13) | data formatting | bytes 524288
